TPU v7x, 512 devices: a whole 4x8x8 slice. The times are simulated.
512 devices in a mesh: dp: 64 (over z, y), tensor: 8 (over x, core).
Axes of the slice: x: 4, y: 8, z: 8, core: 2. Of those that a mesh axis runs over, the one named last changes fastest.
Arguments:
- cache_keys: bfloat16 [3072, 128, 1024], P('dp', None, 'tensor'), may hold values from -5 to 5
- cache_values: bfloat16 [3072, 128, 1024], P('dp', None, 'tensor'), may hold values from -24 to 24
- lengths: int32 [3072], P('dp'), may hold values from 2 to 128, as said below
- queries: bfloat16 [4, 3072, 8192], P(None, 'dp', 'tensor'), may hold values from -125 to 125
- new_keys: bfloat16 [4, 3072, 1024], P(None, 'dp', 'tensor'), may hold values from -9 to 9
- new_values: bfloat16 [4, 3072, 1024], P(None, 'dp', 'tensor'), may hold values from -72 to 72
- reward_weight: bfloat16 [8192], P('tensor'), may hold values from -0.119628906 to 0.119628906
- kept_candidates: int32 [64, 32], P('dp'), may hold values from 0 to 47, as said below
- arrival_cohort: int32 [64, 32], P('dp'), may hold values from 0 to 63, as said below
- arrival_place: int32 [64, 32], P('dp'), may hold values from 0 to 31, as said below
Outputs:
- early_out: bfloat16 [2, 3072, 8192], P(None, 'dp', 'tensor')
- reward: float32 [3072], P('dp')
- late_out: bfloat16 [2, 2048, 8192], P(None, 'dp', 'tensor')
Inputs may be any that keep to these rules, and one draw needn't show every extreme that they name: `kept_candidates`: each row names 32 different candidates of its prompt, in ascending order. `arrival_cohort`: every pair of group and slot receives exactly one survivor. One prompt sends at most 1 survivors to one group, and exactly 1 to some group. `arrival_place`: see arrival_cohort. `lengths`: some candidate holds the full 128 tokens.
All inputs are finite; a program needn't handle non-finite values.
Results may differ from a plain program's by a relative error of at most 0.009.
Values may be sent and summed in bfloat16 or wider, within the bound.
A program may use at most 64 MiB of HBM per device.

v0:
```python
import math

import jax
import jax.numpy as jnp
from jax import lax
from jax.sharding import PartitionSpec as P

HD = 128


def attend(queries_now, key_rows, value_rows, live_length, fresh_k, fresh_v):
    rows_count = queries_now.shape[0]
    cache_rows = key_rows.shape[1]
    seen_steps = fresh_k.shape[1]
    head_width = key_rows.shape[-1]
    groups_here = head_width // HD
    group_size = queries_now.shape[-1] // head_width
    query_b = queries_now.reshape(rows_count, groups_here, group_size, HD)
    key_b = key_rows.reshape(rows_count, cache_rows, groups_here, HD)
    value_b = value_rows.reshape(rows_count, cache_rows, groups_here, HD)
    fresh_kb = fresh_k.reshape(rows_count, seen_steps, groups_here, HD)
    fresh_vb = fresh_v.reshape(rows_count, seen_steps, groups_here, HD)
    score_scale = 1.0 / math.sqrt(HD)
    cache_scores = (
        jnp.einsum("bgqd,bpgd->bgqp", query_b, key_b, preferred_element_type=jnp.float32)
        * score_scale
    )
    fresh_scores = (
        jnp.einsum("bgqd,bngd->bgqn", query_b, fresh_kb, preferred_element_type=jnp.float32)
        * score_scale
    )
    live_rows = jnp.arange(cache_rows, dtype=jnp.int32)[None, :] < live_length[:, None]
    cache_scores = jnp.where(live_rows[:, None, None, :], cache_scores, -jnp.inf)
    row_top = jnp.maximum(jnp.max(cache_scores, axis=-1), jnp.max(fresh_scores, axis=-1))
    cache_exp = jnp.exp(cache_scores - row_top[..., None])
    fresh_exp = jnp.exp(fresh_scores - row_top[..., None])
    row_total = jnp.sum(cache_exp, axis=-1) + jnp.sum(fresh_exp, axis=-1)
    cache_weights = (cache_exp / row_total[..., None]).astype(jnp.bfloat16)
    fresh_weights = (fresh_exp / row_total[..., None]).astype(jnp.bfloat16)
    result = jnp.einsum(
        "bgqp,bpgd->bgqd", cache_weights, value_b, preferred_element_type=jnp.float32
    )
    result = result + jnp.einsum(
        "bgqn,bngd->bgqd", fresh_weights, fresh_vb, preferred_element_type=jnp.float32
    )
    return result.reshape(rows_count, groups_here * group_size * HD).astype(jnp.bfloat16)


def find_row_positions(landed_slot_ids, retained_entries):
    slot_numbers = jnp.arange(retained_entries, dtype=jnp.int32)
    buffer_ids = jnp.arange(landed_slot_ids.shape[0], dtype=jnp.int32)
    matches = landed_slot_ids[None, :] == slot_numbers[:, None]
    return jnp.sum(jnp.where(matches, buffer_ids[None, :], 0), axis=1)


def local(
    cache_keys,
    cache_values,
    lengths,
    queries,
    new_keys,
    new_values,
    reward_weight,
    kept_candidates,
    arrival_cohort,
    arrival_place,
):
    total_steps = queries.shape[0]
    half_steps = total_steps // 2
    fresh_keys = jnp.moveaxis(new_keys, 0, 1)
    fresh_values = jnp.moveaxis(new_values, 0, 1)
    early_list = [
        attend(
            queries[step_index],
            cache_keys,
            cache_values,
            lengths,
            fresh_keys[:, : step_index + 1],
            fresh_values[:, : step_index + 1],
        )
        for step_index in range(half_steps)
    ]
    early_out = jnp.stack(early_list)
    partial_reward = jnp.sum(
        early_out[half_steps - 1].astype(jnp.float32) * reward_weight.astype(jnp.float32), axis=-1
    )
    reward = lax.psum(partial_reward, "tensor")
    group_row_count = lax.axis_size("dp")
    retained_entries = kept_candidates.shape[1]
    slot_capacity = max(1, retained_entries // group_row_count)
    slots_total = group_row_count * slot_capacity
    chosen = kept_candidates[0]
    goal_batch_part = arrival_cohort[0]
    target_place = arrival_place[0]
    champion_spot_number_here = jnp.arange(retained_entries, dtype=jnp.int32)
    same_group = goal_batch_part[:, None] == goal_batch_part[None, :]
    preceding_tally = champion_spot_number_here[None, :] < champion_spot_number_here[:, None]
    order_within = jnp.sum(same_group & preceding_tally, axis=1)
    position = goal_batch_part * slot_capacity + order_within
    buffer_rows = jnp.arange(slots_total, dtype=jnp.int32)
    matchup_lookup = buffer_rows[:, None] == position[None, :]
    occupied = jnp.any(matchup_lookup, axis=1)
    belonging_flags = jnp.sum(
        jnp.where(matchup_lookup, champion_spot_number_here[None, :], 0), axis=1
    )
    slot_sent = jnp.where(occupied, jnp.take(target_place, belonging_flags), -1)
    cand_sent = jnp.take(chosen, belonging_flags)
    send_keys = jnp.take(cache_keys, cand_sent, axis=0)
    send_values = jnp.take(cache_values, cand_sent, axis=0)
    send_queries = jnp.moveaxis(jnp.take(queries[half_steps:], cand_sent, axis=1), 0, 1)
    send_fresh_k = jnp.take(fresh_keys, cand_sent, axis=0)
    send_fresh_v = jnp.take(fresh_values, cand_sent, axis=0)
    send_meta = jnp.stack([jnp.take(lengths, cand_sent), slot_sent], axis=1).astype(jnp.bfloat16)
    landed_rows = (
        lax.all_to_all(send_keys, "dp", split_axis=0, concat_axis=0, tiled=True),
        lax.all_to_all(send_values, "dp", split_axis=0, concat_axis=0, tiled=True),
        lax.all_to_all(send_queries, "dp", split_axis=0, concat_axis=0, tiled=True),
        lax.all_to_all(send_fresh_k, "dp", split_axis=0, concat_axis=0, tiled=True),
        lax.all_to_all(send_fresh_v, "dp", split_axis=0, concat_axis=0, tiled=True),
        lax.all_to_all(send_meta, "dp", split_axis=0, concat_axis=0, tiled=True),
    )
    local_rows = find_row_positions(landed_rows[5][:, 1].astype(jnp.int32), retained_entries)
    keys_here = jnp.take(landed_rows[0], local_rows, axis=0)
    values_here = jnp.take(landed_rows[1], local_rows, axis=0)
    queries_here = jnp.take(landed_rows[2], local_rows, axis=0)
    fresh_k_here = jnp.take(landed_rows[3], local_rows, axis=0)
    fresh_v_here = jnp.take(landed_rows[4], local_rows, axis=0)
    length_here = jnp.take(landed_rows[5][:, 0], local_rows).astype(jnp.int32)
    late_list = [
        attend(
            queries_here[:, step_index - half_steps],
            keys_here,
            values_here,
            length_here,
            fresh_k_here[:, : step_index + 1],
            fresh_v_here[:, : step_index + 1],
        )
        for step_index in range(half_steps, total_steps)
    ]
    late_out = jnp.stack(late_list)
    return (early_out, reward, late_out)


def solution(mesh):
    placed = (
        P("dp", None, "tensor"),
        P("dp", None, "tensor"),
        P("dp"),
        P(None, "dp", "tensor"),
        P(None, "dp", "tensor"),
        P(None, "dp", "tensor"),
        P("tensor"),
        P("dp", None),
        P("dp", None),
        P("dp", None),
    )
    return jax.shard_map(
        local,
        mesh=mesh,
        in_specs=placed,
        out_specs=(P(None, "dp", "tensor"), P("dp"), P(None, "dp", "tensor")),
        check_vma=False,
    )
```

profile of v0, /device:TPU:6, one launch (start us, length us, event | category | flops | bytes accessed | tf_op | source)
XLA Modules:
  0.0 207.7 jit_solution(15865964886168507391)
XLA Ops:
  0.7 1.0 convert_reduce_fusion
  2.5 1.4 gather_fusion.4
  4.0 1.4 gather_fusion
  5.4 1.4 gather_fusion.5
  7.6 16.6 %all-to-all-start = ((bf16[64,1,2]{2,1,0:T(2,128)(2,1)}), bf16[64,1,2]{2,1,0:T(2,128)(2,1)S(1)}, u32[]{:S(2)}, u32[]{:S(2)}) async-start(bf16[64,1,2]{2,1,0:T(2,128)(2,1)} %copy.28), calls=%async_computation | async-start | bytes 65536 | tf_op jit(solution)/shard_map/all_to_all | solution.py:120
  28.6 7.6 %all-to-all-done = bf16[64,1,2]{2,1,0:T(2,128)(2,1)S(1)} async-done(((bf16[64,1,2]{2,1,0:T(2,128)(2,1)}), bf16[64,1,2]{2,1,0:T(2,128)(2,1)S(1)}, u32[]{:S(2)}, u32[]{:S(2)}) %all-to-all-start) | async-done | bytes 288 | tf_op jit(solution)/shard_map/all_to_all | solution.py:120
  36.2 5.1 %all-to-all-start.3 = ((bf16[64,4,128]{2,1,0:T(4,128)(2,1)}), bf16[64,4,128]{2,1,0:T(4,128)(2,1)S(1)}, u32[]{:S(2)}, u32[]{:S(2)}) async-start(bf16[64,4,128]{2,1,0:T(4,128)(2,1)} %get-tuple-element.22), calls=%async_computation.3 | async-start | bytes 131072 | tf_op jit(solution)/shard_map/all_to_all | solution.py:118
  41.5 1.1 gather_fusion.2
  42.6 10.9 %all-to-all-done.3 = bf16[64,4,128]{2,1,0:T(4,128)(2,1)S(1)} async-done(((bf16[64,4,128]{2,1,0:T(4,128)(2,1)}), bf16[64,4,128]{2,1,0:T(4,128)(2,1)S(1)}, u32[]{:S(2)}, u32[]{:S(2)}) %all-to-all-start.3) | async-done | bytes 65568 | tf_op jit(solution)/shard_map/all_to_all | solution.py:118
  53.5 4.6 %all-to-all-start.5 = ((bf16[64,4,128]{2,1,0:T(4,128)(2,1)}), bf16[64,4,128]{2,1,0:T(4,128)(2,1)S(1)}, u32[]{:S(2)}, u32[]{:S(2)}) async-start(bf16[64,4,128]{2,1,0:T(4,128)(2,1)} %get-tuple-element.23), calls=%async_computation.5 | async-start | bytes 131072 | tf_op jit(solution)/shard_map/all_to_all | solution.py:119
  58.1 1.0 broadcast_select_fusion.4
  59.2 11.2 %all-to-all-done.5 = bf16[64,4,128]{2,1,0:T(4,128)(2,1)S(1)} async-done(((bf16[64,4,128]{2,1,0:T(4,128)(2,1)}), bf16[64,4,128]{2,1,0:T(4,128)(2,1)S(1)}, u32[]{:S(2)}, u32[]{:S(2)}) %all-to-all-start.5) | async-done | bytes 65568 | tf_op jit(solution)/shard_map/all_to_all | solution.py:119
  71.0 4.6 %all-to-all-start.1 = ((bf16[64,2,1024]{2,1,0:T(2,128)(2,1)}), bf16[64,2,1024]{2,1,0:T(2,128)(2,1)S(1)}, u32[]{:S(2)}, u32[]{:S(2)}) async-start(bf16[64,2,1024]{2,1,0:T(2,128)(2,1)} %broadcast_select_fusion.4), calls=%async_computation.1 | async-start | bytes 524288 | tf_op jit(solution)/shard_map/all_to_all | solution.py:117
  75.7 2.1 %gather_fusion.6 = bf16[64,128,128]{2,1,0:T(8,128)(2,1)} fusion(bf16[48,128,128]{2,1,0:T(8,128)(2,1)S(1)} %copy-done, s32[1024]{0:T(1024)S(1)} %pad_clamp_fusion.2), kind=kCustom, calls=%fused_computation.1.clone | custom fusion | bytes 4194560 | tf_op jit(solution)/shard_map/jit(_take)/gather | solution.py:108
  77.8 2.1 %gather_fusion.10 = bf16[64,128,128]{2,1,0:T(8,128)(2,1)} fusion(bf16[48,128,128]{2,1,0:T(8,128)(2,1)S(1)} %copy-done.2, s32[1024]{0:T(1024)S(1)} %pad_clamp_fusion.2), kind=kCustom, calls=%fused_computation.6.clone | custom fusion | bytes 4194560 | tf_op jit(solution)/shard_map/jit(_take)/gather | solution.py:109
  79.9 4.7 %broadcast_select_fusion = (bf16[64,128,128]{2,1,0:T(8,128)(2,1)}, bf16[64,128,128]{2,1,0:T(8,128)(2,1)}) fusion(bf16[64,128,128]{2,1,0:T(8,128)(2,1)} %gather_fusion.10, pred[64]{0:T(512)(128)(4,1)S(1)} %get-tuple-element.12, bf16[64,128,128]{2,1,0:T(8,128)(2,1)} %gather_fusion.6), kind=kLoop, calls=%fused_computation.14 | loop fusion | flops 2097152 | bytes 8388672 | tf_op jit(solution)/shard_map/jit(_take)/select_n | solution.py:109
  84.6 4.7 %all-to-all-done.1 = bf16[64,2,1024]{2,1,0:T(2,128)(2,1)S(1)} async-done(((bf16[64,2,1024]{2,1,0:T(2,128)(2,1)}), bf16[64,2,1024]{2,1,0:T(2,128)(2,1)S(1)}, u32[]{:S(2)}, u32[]{:S(2)}) %all-to-all-start.1) | async-done | bytes 262176 | tf_op jit(solution)/shard_map/all_to_all | solution.py:117
  89.9 8.4 %all-to-all-start.2 = ((bf16[64,128,128]{2,1,0:T(8,128)(2,1)}), bf16[64,128,128]{2,1,0:T(8,128)(2,1)}, u32[]{:S(2)}, u32[]{:S(2)}) async-start(bf16[64,128,128]{2,1,0:T(8,128)(2,1)} %get-tuple-element.19), calls=%async_computation.2 | async-start | bytes 4194304 | tf_op jit(solution)/shard_map/all_to_all | solution.py:115
  98.6 1.0 fusion.50
  99.6 1.0 fusion.49
  101.8 1.0 fusion.51
  104.1 42.7 %all-to-all-done.2 = bf16[64,128,128]{2,1,0:T(8,128)(2,1)} async-done(((bf16[64,128,128]{2,1,0:T(8,128)(2,1)}), bf16[64,128,128]{2,1,0:T(8,128)(2,1)}, u32[]{:S(2)}, u32[]{:S(2)}) %all-to-all-start.2) | async-done | bytes 2097184 | tf_op jit(solution)/shard_map/all_to_all | solution.py:115
  146.8 8.9 %all-to-all-start.4 = ((bf16[64,128,128]{2,1,0:T(8,128)(2,1)}), bf16[64,128,128]{2,1,0:T(8,128)(2,1)}, u32[]{:S(2)}, u32[]{:S(2)}) async-start(bf16[64,128,128]{2,1,0:T(8,128)(2,1)} %get-tuple-element.18), calls=%async_computation.4 | async-start | bytes 4194304 | tf_op jit(solution)/shard_map/all_to_all | solution.py:116
  156.6 0.8 fusion.40
  157.4 2.0 fusion.2
  159.4 0.9 convert_element_type.123
  160.4 11.3 %psum.7 = f32[48]{0:T(128)} all-reduce(f32[48]{0:T(128)S(1)} %get-tuple-element.32), channel_id=1, replica_groups=mesh['dp'=64,'tensor'=8] {'tensor'}, use_global_device_ids=true, to_apply=%region_7.8 | all-reduce | flops 48 | bytes 384 | tf_op jit(solution)/shard_map/psum | solution.py:87
  174.0 1.4 gather_fusion.13
  175.6 1.8 gather_fusion.3
  178.6 2.3 %gather_fusion.7 = bf16[32,128,128]{2,1,0:T(8,128)(2,1)S(1)} fusion(bf16[64,128,128]{2,1,0:T(8,128)(2,1)} %all-to-all-done.2, s32[1024]{0:T(1024)S(1)} %pad_clamp_fusion), kind=kCustom, calls=%fused_computation.2.clone | custom fusion | bytes 2097280 | tf_op jit(solution)/shard_map/jit(_take)/gather | solution.py:123
  183.0 20.1 %all-to-all-done.4 = bf16[64,128,128]{2,1,0:T(8,128)(2,1)} async-done(((bf16[64,128,128]{2,1,0:T(8,128)(2,1)}), bf16[64,128,128]{2,1,0:T(8,128)(2,1)}, u32[]{:S(2)}, u32[]{:S(2)}) %all-to-all-start.4) | async-done | bytes 2097184 | tf_op jit(solution)/shard_map/all_to_all | solution.py:116
  203.1 2.3 %gather_fusion.11 = bf16[32,128,128]{2,1,0:T(8,128)(2,1)S(1)} fusion(bf16[64,128,128]{2,1,0:T(8,128)(2,1)} %all-to-all-done.4, s32[1024]{0:T(1024)S(1)} %pad_clamp_fusion), kind=kCustom, calls=%fused_computation.7.clone | custom fusion | bytes 2097280 | tf_op jit(solution)/shard_map/jit(_take)/gather | solution.py:124
  (107 shorter events, 18.7 us)
Async XLA Ops:
  0.6 75.0 %copy-start = (bf16[48,128,128]{2,1,0:T(8,128)(2,1)S(1)}, bf16[48,128,128]{2,1,0:T(8,128)(2,1)}, u32[]{:S(2)}) copy-start(bf16[48,128,128]{2,1,0:T(8,128)(2,1)} %param.20) | copy-start | bytes 4718596
  0.6 40.7 %slice-start = ((bf16[4,48,1024]{2,1,0:T(8,128)(2,1)}), bf16[2,48,1024]{2,1,0:T(8,128)(2,1)S(1)}, s32[]{:S(2)}) async-start(bf16[4,48,1024]{2,1,0:T(8,128)(2,1)} %param.23), calls=%async_computation.6 | async-start | bytes 393216 | tf_op jit(solution)/shard_map/slice | solution.py:110
  7.6 28.6 %all-to-all-start = ((bf16[64,1,2]{2,1,0:T(2,128)(2,1)}), bf16[64,1,2]{2,1,0:T(2,128)(2,1)S(1)}, u32[]{:S(2)}, u32[]{:S(2)}) async-start(bf16[64,1,2]{2,1,0:T(2,128)(2,1)} %copy.28), calls=%async_computation | async-start | bytes 65536 | tf_op jit(solution)/shard_map/all_to_all | solution.py:120
  25.0 0.6 copy-start.7
  27.1 14.2 %copy-start.5 = (bf16[4,48,128]{2,0,1:T(4,128)(2,1)}, bf16[4,48,128]{2,0,1:T(4,128)(2,1)S(1)}, u32[]{:S(2)}) copy-start(bf16[4,48,128]{2,0,1:T(4,128)(2,1)S(1)} %copy.40) | copy-start | bytes 147460
  36.2 5.1 %copy-start.13 = (bf16[64,1,2]{2,1,0:T(2,128)(2,1)}, bf16[64,1,2]{2,1,0:T(2,128)(2,1)S(1)}, u32[]{:S(2)}) copy-start(bf16[64,1,2]{2,1,0:T(2,128)(2,1)S(1)} %all-to-all-done) | copy-start | bytes 772
  36.2 17.3 %all-to-all-start.3 = ((bf16[64,4,128]{2,1,0:T(4,128)(2,1)}), bf16[64,4,128]{2,1,0:T(4,128)(2,1)S(1)}, u32[]{:S(2)}, u32[]{:S(2)}) async-start(bf16[64,4,128]{2,1,0:T(4,128)(2,1)} %get-tuple-element.22), calls=%async_computation.3 | async-start | bytes 131072 | tf_op jit(solution)/shard_map/all_to_all | solution.py:118
  53.5 16.9 %copy-start.10 = (bf16[64,4,128]{2,1,0:T(4,128)(2,1)}, bf16[64,4,128]{2,1,0:T(4,128)(2,1)S(1)}, u32[]{:S(2)}) copy-start(bf16[64,4,128]{2,1,0:T(4,128)(2,1)S(1)} %all-to-all-done.3) | copy-start | bytes 196612
  53.5 16.9 %all-to-all-start.5 = ((bf16[64,4,128]{2,1,0:T(4,128)(2,1)}), bf16[64,4,128]{2,1,0:T(4,128)(2,1)S(1)}, u32[]{:S(2)}, u32[]{:S(2)}) async-start(bf16[64,4,128]{2,1,0:T(4,128)(2,1)} %get-tuple-element.23), calls=%async_computation.5 | async-start | bytes 131072 | tf_op jit(solution)/shard_map/all_to_all | solution.py:119
  70.4 0.6 copy-start.12
  71.0 18.2 %all-to-all-start.1 = ((bf16[64,2,1024]{2,1,0:T(2,128)(2,1)}), bf16[64,2,1024]{2,1,0:T(2,128)(2,1)S(1)}, u32[]{:S(2)}, u32[]{:S(2)}) async-start(bf16[64,2,1024]{2,1,0:T(2,128)(2,1)} %broadcast_select_fusion.4), calls=%async_computation.1 | async-start | bytes 524288 | tf_op jit(solution)/shard_map/all_to_all | solution.py:117
  75.6 2.2 %copy-start.2 = (bf16[48,128,128]{2,1,0:T(8,128)(2,1)S(1)}, bf16[48,128,128]{2,1,0:T(8,128)(2,1)}, u32[]{:S(2)}) copy-start(bf16[48,128,128]{2,1,0:T(8,128)(2,1)} %param.21) | copy-start | bytes 4718596
  89.2 0.7 copy-start.4
  89.9 8.5 %copy-start.3 = (bf16[4,48,1024]{2,1,0:T(8,128)(2,1)S(1)}, bf16[4,48,1024]{2,1,0:T(8,128)(2,1)}, u32[]{:S(2)}) copy-start(bf16[4,48,1024]{2,1,0:T(8,128)(2,1)} %param.23) | copy-start | bytes 1179652
  89.9 8.6 %copy-start.1 = (s32[48]{0:T(128)S(1)}, s32[48]{0:T(128)}, u32[]{:S(2)}) copy-start(s32[48]{0:T(128)} %param.22) | copy-start | bytes 580
  89.9 56.8 %all-to-all-start.2 = ((bf16[64,128,128]{2,1,0:T(8,128)(2,1)}), bf16[64,128,128]{2,1,0:T(8,128)(2,1)}, u32[]{:S(2)}, u32[]{:S(2)}) async-start(bf16[64,128,128]{2,1,0:T(8,128)(2,1)} %get-tuple-element.19), calls=%async_computation.2 | async-start | bytes 4194304 | tf_op jit(solution)/shard_map/all_to_all | solution.py:115
  98.4 2.5 %copy-start.17 = (bf16[1024]{0:T(1024)(128)(2,1)S(1)}, bf16[1024]{0:T(1024)(128)(2,1)}, u32[]{:S(2)}) copy-start(bf16[1024]{0:T(1024)(128)(2,1)} %param.26) | copy-start | bytes 6148
  98.4 2.5 %copy-start.6 = (bf16[4,48,128]{2,0,1:T(4,128)(2,1)S(1)}, bf16[4,48,128]{2,0,1:T(4,128)(2,1)}, u32[]{:S(2)}) copy-start(bf16[4,48,128]{2,0,1:T(4,128)(2,1)} %copy-done.5) | copy-start | bytes 147460
  98.4 3.2 %copy-start.8 = (bf16[4,48,128]{2,0,1:T(4,128)(2,1)S(1)}, bf16[4,48,128]{2,0,1:T(4,128)(2,1)}, u32[]{:S(2)}) copy-start(bf16[4,48,128]{2,0,1:T(4,128)(2,1)} %copy-done.7) | copy-start | bytes 147460
  101.7 1.3 copy-start.15
  102.8 0.6 copy-start.9
  102.8 52.9 %copy-start.16 = (f32[48,8]{1,0:T(8,128)}, f32[48,8]{1,0:T(8,128)S(1)}, u32[]{:S(2)}) copy-start(f32[48,8]{1,0:T(8,128)S(1)} %multiply_maximum_fusion) | copy-start | bytes 4612
  146.8 56.3 %all-to-all-start.4 = ((bf16[64,128,128]{2,1,0:T(8,128)(2,1)}), bf16[64,128,128]{2,1,0:T(8,128)(2,1)}, u32[]{:S(2)}, u32[]{:S(2)}) async-start(bf16[64,128,128]{2,1,0:T(8,128)(2,1)} %get-tuple-element.18), calls=%async_computation.4 | async-start | bytes 4194304 | tf_op jit(solution)/shard_map/all_to_all | solution.py:116
  156.6 15.8 %copy-start.14 = (bf16[64,1,2]{2,1,0:T(2,128)(2,1)S(1)}, bf16[64,1,2]{2,1,0:T(2,128)(2,1)}, u32[]{:S(2)}) copy-start(bf16[64,1,2]{2,1,0:T(2,128)(2,1)} %copy-done.13) | copy-start | bytes 772
  156.6 16.8 %copy-start.11 = (bf16[64,4,128]{2,1,0:T(4,128)(2,1)S(1)}, bf16[64,4,128]{2,1,0:T(4,128)(2,1)}, u32[]{:S(2)}) copy-start(bf16[64,4,128]{2,1,0:T(4,128)(2,1)} %copy-done.10) | copy-start | bytes 196612
where the time goes:
time: 211 us; the launch traced here: 208 us
  waiting for transfers between devices  97.2 us (46%)
  starting transfers between devices  48.3 us (23%)
  local copies, waits for them, and re-layouts  26.8 us (13%)
  other arithmetic  13.4 us (6%)
  blocking collectives  11.3 us (5%)
  matrix products  9.43 us (4%)
    all_to_all x1, waiting for transfers between devices, local(): lax.all_to_all(send_keys, 'dp', split_axis=0, concat_axis=0, tiled=True)  42.7 us
    all_to_all x1, waiting for transfers between devices, local(): lax.all_to_all(send_values, 'dp', split_axis=0, concat_axis=0, tiled=True)  20.1 us
    all_to_all x1, starting transfers between devices, local(): lax.all_to_all(send_meta, 'dp', split_axis=0, concat_axis=0, tiled=True)  16.6 us
    psum x1, blocking collectives, local(): reward = lax.psum(partial_reward, 'tensor')  11.3 us
    all_to_all x1, waiting for transfers between devices, local(): lax.all_to_all(send_fresh_v, 'dp', split_axis=0, concat_axis=0, tiled=True)  11.2 us
    all_to_all x1, waiting for transfers between devices, local(): lax.all_to_all(send_fresh_k, 'dp', split_axis=0, concat_axis=0, tiled=True)  10.9 us
    all_to_all x1, starting transfers between devices, local(): lax.all_to_all(send_values, 'dp', split_axis=0, concat_axis=0, tiled=True)  8.94 us
    all_to_all x1, starting transfers between devices, local(): lax.all_to_all(send_keys, 'dp', split_axis=0, concat_axis=0, tiled=True)  8.44 us
  transfers between devices with their start and end apart: 6, of which 6 were waited for; matrix products, arithmetic and copies ran while one was open for 17% of the time, Pallas kernels for 0%

commit v1 on v0

v1 whole, which is shorter than its diff:
```python
import functools
import math

import jax
import jax.numpy as jnp
from jax import lax
from jax.experimental import pallas as pl
from jax.experimental.pallas import tpu as pltpu
from jax.sharding import PartitionSpec as P

MESH = pl.DeviceIdType.MESH
HD = 128
PAD = 16
BLOCK = 8
RING = 8
NEG = -1e30
NT = (((1,), (1,)), ((), ()))


def all_of(ref, count, sem):
    part = ref.at[pl.ds(0, count)]
    return pltpu.make_async_copy(part, part, sem)


def kernel(
    dims,
    kept_s, lengths_s, cohort_v, place_v, weight_v,
    keys_h, values_h, queries_h, fresh_k_h, fresh_v_h,
    early_h, reward_o, late_h,
    kx, vx, qb, nkb, nvb, qf, nf, of, late_buf, send, recv, stage, late_stage,
    row_v, idx_s, meta_mine, meta_y, meta_all, rw,
    in_sem, row_sem, out_sem, send_sem, recv_sem, my_send, my_recv, mz_send, mz_recv,
    rw_send, rw_recv,
):
    zn, yn, tn, cand, kept_n, heads = dims
    groups = zn * yn
    cache = kx.shape[1] - PAD
    g_me = lax.axis_index("dp")
    t_me = lax.axis_index("tensor")
    z_me, y_me = g_me // yn, g_me % yn

    ins = [
        pltpu.make_async_copy(queries_h, qb, in_sem.at[0]),
        pltpu.make_async_copy(fresh_k_h, nkb, in_sem.at[1]),
        pltpu.make_async_copy(fresh_v_h, nvb, in_sem.at[2]),
        pltpu.make_async_copy(keys_h, kx.at[:, pl.ds(0, cache), :], in_sem.at[3]),
        pltpu.make_async_copy(values_h, vx.at[:, pl.ds(0, cache), :], in_sem.at[4]),
    ]
    for copy in ins:
        copy.start()

    barrier = pltpu.get_barrier_semaphore()

    def greet(d, _):
        pl.semaphore_signal(
            barrier, inc=1, device_id=(lax.rem(g_me + d, groups), t_me), device_id_type=MESH
        )
        return 0

    lax.fori_loop(1, groups, greet, 0)

    def greet_t(d, _):
        pl.semaphore_signal(
            barrier, inc=1, device_id=(g_me, lax.rem(t_me + d, tn)), device_id_type=MESH
        )
        return 0

    lax.fori_loop(1, tn, greet_t, 0)

    eye = lax.broadcasted_iota(jnp.int32, (kept_n, kept_n), 0) == lax.broadcasted_iota(
        jnp.int32, (kept_n, kept_n), 1
    )

    def column(row):
        return jnp.sum(jnp.where(eye, row, 0), axis=1, keepdims=True)

    lane_g = lax.broadcasted_iota(jnp.int32, (kept_n, 128), 1)
    sub_k = lax.broadcasted_iota(jnp.int32, (kept_n, 128), 0)
    hit = column(cohort_v[...]) == lane_g
    chosen = jnp.min(jnp.where(hit, sub_k, kept_n), axis=0, keepdims=True)
    slot_row = jnp.max(jnp.where(hit, column(place_v[...]) + 1, 0), axis=0, keepdims=True)
    row_v[0] = chosen
    to_smem = pltpu.make_async_copy(row_v.at[0], idx_s.at[0], row_sem.at[0])
    to_smem.start()
    meta_mine[...] = jnp.where(
        lax.broadcasted_iota(jnp.int32, (RING, 128), 0) == y_me, slot_row, 0
    )

    pl.semaphore_wait(barrier, groups - 1 + tn - 1)

    def y_copy(d):
        return pltpu.make_async_remote_copy(
            src_ref=meta_mine,
            dst_ref=meta_y.at[y_me],
            send_sem=my_send,
            recv_sem=my_recv,
            device_id=(z_me * yn + lax.rem(y_me + d, yn), t_me),
            device_id_type=MESH,
        )

    lax.fori_loop(1, yn, lambda d, _: (y_copy(d).start(), 0)[1], 0)
    meta_y[y_me] = meta_mine[...]

    for copy in ins[:3]:
        copy.wait()
    steps = qb.shape[0]
    for t in range(steps):
        for h in range(heads):
            qf[pl.ds((t * heads + h) * cand, cand), :] = qb[
                t, :, h * HD : (h + 1) * HD
            ].astype(jnp.float32)
    for which, source in enumerate((nkb, nvb)):
        for t in range(steps):
            nf[which, pl.ds(t * cand, cand), :] = source[t].astype(jnp.float32)
        nf[which, pl.ds(steps * cand, (8 - steps) * cand), :] = jnp.zeros(
            ((8 - steps) * cand, HD), jnp.float32
        )
    empty = jnp.zeros((PAD - 8, HD), jnp.float32)
    for c in range(cand):
        for which, target in enumerate((kx, vx)):
            rows = nf[which, pl.ds(c, 8, stride=cand), :]
            target[c, pl.ds(cache, PAD), :] = jnp.concatenate([rows, empty], axis=0).astype(
                jnp.bfloat16
            )
    for copy in ins[3:]:
        copy.wait()

    width = cache + PAD
    lane = lax.broadcasted_iota(jnp.int32, (2 * heads, width), 1)
    step_of_row = lax.broadcasted_iota(jnp.int32, (2 * heads, width), 0) // heads
    rate = math.log2(math.e) / math.sqrt(HD)

    def attend(cands, first_step):
        fresh_seen = (lane >= cache) & (lane <= cache + first_step + step_of_row)
        scores = []
        for c in cands:
            q = jnp.concatenate(
                [
                    qf[pl.ds((first_step + i) * heads * cand + c, heads, stride=cand), :]
                    for i in range(2)
                ],
                axis=0,
            ).astype(jnp.bfloat16)
            s = lax.dot_general(q, kx[c], NT, preferred_element_type=jnp.float32)
            scores.append(jnp.where((lane < lengths_s[c]) | fresh_seen, s, NEG))
        tops = [jnp.max(s, axis=1, keepdims=True) for s in scores]
        weights = [jnp.exp2((s - m) * rate) for s, m in zip(scores, tops)]
        totals = [jnp.sum(w, axis=1, keepdims=True) for w in weights]
        return [
            jnp.dot(w.astype(jnp.bfloat16), vx[c], preferred_element_type=jnp.float32)
            / total
            for c, w, total in zip(cands, weights, totals)
        ]

    def late_block(b, _):
        cands = [kept_s[0, b * BLOCK + j] for j in range(BLOCK)]
        outs = attend(cands, steps // 2)
        for j, o in enumerate(outs):
            late_buf[b * BLOCK + j] = o.astype(jnp.bfloat16)
        return 0

    late_buf[kept_n] = jnp.zeros(late_buf.shape[1:], jnp.bfloat16)
    lax.fori_loop(0, kept_n // BLOCK, late_block, 0)

    for sem in (my_send, my_recv):
        all_of(meta_y, yn - 1, sem).wait()
    meta_all[z_me] = jnp.sum(meta_y[...], axis=0)

    def z_copy(d):
        return pltpu.make_async_remote_copy(
            src_ref=meta_all.at[z_me],
            dst_ref=meta_all.at[z_me],
            send_sem=mz_send,
            recv_sem=mz_recv,
            device_id=(lax.rem(z_me + d, zn) * yn + y_me, t_me),
            device_id_type=MESH,
        )

    lax.fori_loop(1, zn, lambda d, _: (z_copy(d).start(), 0)[1], 0)

    to_smem.wait()
    for g in range(groups):
        send[g] = late_buf[idx_s[0, 0, g]]

    def row_copy(d):
        g = lax.rem(g_me + d, groups)
        return pltpu.make_async_remote_copy(
            src_ref=send.at[g],
            dst_ref=recv.at[g_me],
            send_sem=send_sem,
            recv_sem=recv_sem,
            device_id=(g, t_me),
            device_id_type=MESH,
        )

    lax.fori_loop(1, groups, lambda d, _: (row_copy(d).start(), 0)[1], 0)
    recv[g_me] = send[g_me]

    def early_block(b, _):
        cands = [b * BLOCK + j for j in range(BLOCK)]
        outs = attend(cands, 0)
        for c, o in zip(cands, outs):
            for i in range(2):
                of[pl.ds(i * heads * cand + c, heads, stride=cand), :] = o[
                    i * heads : (i + 1) * heads
                ]
        return 0

    lax.fori_loop(0, cand // BLOCK, early_block, 0)
    for t in range(2):
        for h in range(heads):
            stage[t, :, h * HD : (h + 1) * HD] = of[
                pl.ds((t * heads + h) * cand, cand), :
            ].astype(jnp.bfloat16)
    early_copy = pltpu.make_async_copy(stage, early_h, out_sem.at[0])
    early_copy.start()
    rw[t_me] = jnp.zeros(rw.shape[1:], jnp.float32)
    rw[t_me, :, pl.ds(0, cand)] = lax.dot_general(
        weight_v[...], stage[1], NT, preferred_element_type=jnp.float32
    )

    def rw_copy(d):
        return pltpu.make_async_remote_copy(
            src_ref=rw.at[t_me],
            dst_ref=rw.at[t_me],
            send_sem=rw_send,
            recv_sem=rw_recv,
            device_id=(g_me, lax.rem(t_me + d, tn)),
            device_id_type=MESH,
        )

    lax.fori_loop(1, tn, lambda d, _: (rw_copy(d).start(), 0)[1], 0)

    if zn > 1:
        for sem in (mz_send, mz_recv):
            all_of(meta_all, zn - 1, sem).wait()
    met = meta_all[...].reshape(zn * RING, 128)
    lane_m = lax.broadcasted_iota(jnp.int32, (zn * RING, 128), 1)
    sub_m = lax.broadcasted_iota(jnp.int32, (zn * RING, 128), 0)
    slots_here = jnp.sum(jnp.where(lane_m == g_me, met, 0), axis=1, keepdims=True)
    sender = (sub_m // RING) * yn + sub_m % RING
    row_v[1] = jnp.max(
        jnp.where(slots_here == lane_m + 1, sender, 0), axis=0, keepdims=True
    )
    back = pltpu.make_async_copy(row_v.at[1], idx_s.at[1], row_sem.at[1])
    back.start()
    back.wait()

    for sem in (send_sem, recv_sem):
        all_of(recv, groups - 1, sem).wait()
    for p in range(kept_n):
        o = recv[idx_s[1, 0, p]].astype(jnp.float32)
        for i in range(2):
            of[pl.ds(i * heads * kept_n + p, heads, stride=kept_n), :] = o[
                i * heads : (i + 1) * heads
            ]
    for t in range(2):
        for h in range(heads):
            late_stage[t, :, h * HD : (h + 1) * HD] = of[
                pl.ds((t * heads + h) * kept_n, kept_n), :
            ].astype(jnp.bfloat16)
    late_copy = pltpu.make_async_copy(late_stage, late_h, out_sem.at[1])
    late_copy.start()
    if tn > 1:
        for sem in (rw_send, rw_recv):
            all_of(rw, tn - 1, sem).wait()
    reward_o[...] = jnp.sum(rw[...], axis=0)[:, :cand]
    early_copy.wait()
    late_copy.wait()


def local(
    ring,
    tn,
    cache_keys,
    cache_values,
    lengths,
    queries,
    new_keys,
    new_values,
    reward_weight,
    kept_candidates,
    arrival_cohort,
    arrival_place,
):
    zn, yn = ring
    groups = zn * yn
    cand, cache, _ = cache_keys.shape
    steps, _, columns = queries.shape
    heads = columns // HD
    kept_n = kept_candidates.shape[1]
    half = steps // 2
    bf16, f32, i32 = jnp.bfloat16, jnp.float32, jnp.int32
    smem = pl.BlockSpec(memory_space=pltpu.SMEM)
    vmem = pl.BlockSpec(memory_space=pltpu.VMEM)
    hbm = pl.BlockSpec(memory_space=pl.ANY)
    dma = pltpu.SemaphoreType.DMA
    early, reward, late = pl.pallas_call(
        functools.partial(kernel, (zn, yn, tn, cand, kept_n, heads)),
        out_shape=(
            jax.ShapeDtypeStruct((half, cand, columns), bf16),
            jax.ShapeDtypeStruct((1, cand), f32),
            jax.ShapeDtypeStruct((half, kept_n, columns), bf16),
        ),
        in_specs=[smem, smem, vmem, vmem, vmem, hbm, hbm, hbm, hbm, hbm],
        out_specs=(hbm, vmem, hbm),
        scratch_shapes=[
            pltpu.VMEM((cand, cache + PAD, HD), bf16),
            pltpu.VMEM((cand, cache + PAD, HD), bf16),
            pltpu.VMEM(queries.shape, bf16),
            pltpu.VMEM(new_keys.shape, bf16),
            pltpu.VMEM(new_values.shape, bf16),
            pltpu.VMEM((steps * heads * cand, HD), f32),
            pltpu.VMEM((2, 8 * cand, HD), f32),
            pltpu.VMEM((half * heads * cand, HD), f32),
            pltpu.VMEM((kept_n + 1, half * heads, HD), bf16),
            pltpu.VMEM((groups, half * heads, HD), bf16),
            pltpu.VMEM((groups, half * heads, HD), bf16),
            pltpu.VMEM((half, cand, columns), bf16),
            pltpu.VMEM((half, kept_n, columns), bf16),
            pltpu.VMEM((2, 1, 128), i32),
            pltpu.SMEM((2, 1, 128), i32),
            pltpu.VMEM((RING, 128), i32),
            pltpu.VMEM((yn, RING, 128), i32),
            pltpu.VMEM((zn, RING, 128), i32),
            pltpu.VMEM((tn, 1, 128), f32),
            dma((5,)), dma((2,)), dma((2,)),
            dma, dma, dma, dma, dma, dma, dma, dma,
        ],
        compiler_params=pltpu.CompilerParams(
            collective_id=0, has_side_effects=True, vmem_limit_bytes=60 * 1024 * 1024
        ),
    )(
        kept_candidates,
        lengths,
        arrival_cohort,
        arrival_place,
        reward_weight.reshape(1, columns),
        cache_keys,
        cache_values,
        queries,
        new_keys,
        new_values,
    )
    return early, reward.reshape(cand), late


def solution(mesh):
    groups, tn = mesh.shape["dp"], mesh.shape["tensor"]
    yn = min(RING, groups)
    placed = (
        P("dp", None, "tensor"),
        P("dp", None, "tensor"),
        P("dp"),
        P(None, "dp", "tensor"),
        P(None, "dp", "tensor"),
        P(None, "dp", "tensor"),
        P("tensor"),
        P("dp", None),
        P("dp", None),
        P("dp", None),
    )
    return jax.shard_map(
        functools.partial(local, (groups // yn, yn), tn),
        mesh=mesh,
        in_specs=placed,
        out_specs=(P(None, "dp", "tensor"), P("dp"), P(None, "dp", "tensor")),
        check_vma=False,
    )
```

time: 211 us -> 38.2 us (0.18); the launches traced: 208 us -> 38 us
  waiting for transfers between devices: 97.2 us -> 0 us
  starting transfers between devices: 48.3 us -> 0 us
  Pallas kernels: 0 us -> 31.8 us
  local copies, waits for them, and re-layouts: 26.8 us -> 5.58 us
  other arithmetic: 13.4 us -> 0 us
  blocking collectives: 11.3 us -> 0 us
  matrix products: 9.43 us -> 0 us
    all_to_all x6 -> x0, waiting for transfers between devices: 97.2 us -> none  [the longest x1 42.7 us: local(): lax.all_to_all(send_keys, 'dp', split_axis=0, concat_axis=0, tiled=True)]
    all_to_all x6 -> x0, starting transfers between devices: 48.3 us -> none  [the longest x1 16.6 us: local(): lax.all_to_all(send_meta, 'dp', split_axis=0, concat_axis=0, tiled=True)]
    pallas_call x0 -> x1, Pallas kernels: none -> 31.8 us  [local(): pl.pallas_call(functools.partial(kernel, (zn, yn, tn, cand, kept_n, heads...]
    gather x14 -> x0, local copies, waits for them, and re-layouts: 20.2 us -> none  [the longest x1 2.34 us: local(): keys_here = jnp.take(landed_rows[0], local_rows, axis=0)]
    psum x1 -> x0, blocking collectives: 11.3 us -> none  [local(): reward = lax.psum(partial_reward, 'tensor')]
    dot_general x15 -> x0, matrix products: 9.43 us -> none  [the longest x4 3.6 us: attend(): jnp.einsum('bgqp,bpgd->bgqd', cache_weights, value_b, preferred_element_t...]
    select_n x8 -> x0, other arithmetic: 6.79 us -> none  [the longest x1 4.65 us: local(): send_values = jnp.take(cache_values, cand_sent, axis=0)]
    reduce_sum x10 -> x0, other arithmetic: 2.78 us -> none  [the longest x7 1.6 us: attend(): row_total = jnp.sum(cache_exp, axis=-1) + jnp.sum(fresh_exp, axis=-1)]
  transfers between devices with their start and end apart: 6 -> 0, of which waited for: 6 -> 0; matrix products, arithmetic and copies ran while one was open for 17% -> 0% of each run, Pallas kernels for 0% -> 0%
where the time goes in v1:
time: 38.2 us; the launch traced here: 38 us
  Pallas kernels  31.8 us (83%)
  local copies, waits for them, and re-layouts  5.58 us (15%)
  between operations  0.64 us (2%)
    pallas_call x1, Pallas kernels, local(): pl.pallas_call(functools.partial(kernel, (zn, yn, tn, cand, kept_n, heads...  31.8 us
    unnamed x3, local copies, waits for them, and re-layouts  4.3 us
    reshape x1, local copies, waits for them, and re-layouts, local(): reward_weight.reshape(1, columns)  1.28 us

profile of v1, /device:TPU:6, one launch (start us, length us, event | category | flops | bytes accessed | tf_op | source)
XLA Modules:
  0.0 38.0 jit_solution(4586995436797941018)
XLA Ops:
  0.6 1.3 %reshape.12.weight_v = bf16[1,1024]{1,0:T(2,128)(2,1)} reshape(bf16[1024]{0:T(1024)(128)(2,1)} %param.16) | data formatting | bytes 4096 | tf_op jit(solution)/shard_map/reshape | solution.py:338
  1.9 31.8 %shard_map.121 = (bf16[2,48,1024]{2,1,0:T(8,128)(2,1)}, f32[1,48]{1,0:T(1,128)}, bf16[2,32,1024]{2,1,0:T(8,128)(2,1)}) custom-call(s32[1,32]{1,0:T(1,128)} %kept_s.1, s32[48]{0:T(128)} %lengths_s.1, s32[1,32]{1,0:T(1,128)} %cohort_v.1, s32[1,32]{1,0:T(1,128)} %place_v.1, bf16[1,1024]{1,0:T(2,128)(2,1)} %reshape.12.weight_v, bf16[48,128,128]{2,1,0:T(8,128)(2,1)} %keys_h.1, ...), custom_call_target="tpu_custom_call" | custom-call | tf_op jit(solution)/shard_map/pallas_call | solution.py:298
  33.7 1.6 %copy.16 = bf16[2,48,1024]{2,1,0:T(8,128)(2,1)} copy(bf16[2,48,1024]{2,1,0:T(8,128)(2,1)} %get-tuple-element.12) | data formatting | bytes 393216
  35.3 1.1 %copy.17 = f32[48]{0:T(128)} copy(f32[48]{0:T(128)} %bitcast.1) | data formatting | bytes 384
  36.4 1.6 %copy.18 = bf16[2,32,1024]{2,1,0:T(8,128)(2,1)} copy(bf16[2,32,1024]{2,1,0:T(8,128)(2,1)} %get-tuple-element.14) | data formatting | bytes 262144

commit v2 on v1

v2 whole, which is shorter than its diff:
```python
import functools
import math

import jax
import jax.numpy as jnp
from jax import lax
from jax.experimental import pallas as pl
from jax.experimental.pallas import tpu as pltpu
from jax.sharding import PartitionSpec as P

MESH = pl.DeviceIdType.MESH
HD = 128
PAD = 16
BLOCK = 8
RING = 8
NEG = -1e30
NT = (((1,), (1,)), ((), ()))


def all_of(ref, count, sem):
    part = ref.at[pl.ds(0, count)]
    return pltpu.make_async_copy(part, part, sem)


def kernel(
    dims,
    kept_h, lengths_h, cohort_h, place_h, weight_h,
    keys_h, values_h, queries_h, fresh_k_h, fresh_v_h,
    stage, reward_o, late_stage,
    kept_s, lengths_s, cohort_v, place_v, weight_v,
    kx, vx, qb, nkb, nvb, qf, nf, of, late_buf, send, recv,
    row_v, idx_s, meta_mine, meta_all, rw,
    in_sem, row_sem, send_sem, recv_sem, meta_send, meta_recv, rw_send, rw_recv,
):
    zn, yn, tn, cand, kept_n, heads = dims
    groups = zn * yn
    cache = kx.shape[1] - PAD
    g_me = lax.axis_index("dp")
    t_me = lax.axis_index("tensor")
    z_me, y_me = g_me // yn, g_me % yn

    def hops(offset):
        return min(offset[0], zn - offset[0]) + min(offset[1], yn - offset[1])

    others = sorted(((i, j) for i in range(zn) for j in range(yn)), key=hops)[:0:-1]
    others = [
        lax.rem(z_me + i, zn) * yn + lax.rem(y_me + j, yn) for i, j in others
    ]

    ins = [
        pltpu.make_async_copy(src, dst, in_sem.at[i])
        for i, (src, dst) in enumerate(
            (
                (cohort_h, cohort_v),
                (place_h, place_v),
                (fresh_k_h, nkb),
                (fresh_v_h, nvb),
                (queries_h, qb),
                (kept_h, kept_s),
                (lengths_h, lengths_s),
                (keys_h, kx.at[:, pl.ds(0, cache), :]),
                (values_h, vx.at[:, pl.ds(0, cache), :]),
                (weight_h, weight_v),
            )
        )
    ]
    for copy in ins:
        copy.start()

    barrier = pltpu.get_barrier_semaphore()

    for g in others:
        pl.semaphore_signal(barrier, inc=1, device_id=(g, t_me), device_id_type=MESH)

    def greet_t(d, _):
        pl.semaphore_signal(
            barrier, inc=1, device_id=(g_me, lax.rem(t_me + d, tn)), device_id_type=MESH
        )
        return 0

    lax.fori_loop(1, tn, greet_t, 0)

    for copy in ins[:2]:
        copy.wait()

    eye = lax.broadcasted_iota(jnp.int32, (kept_n, kept_n), 0) == lax.broadcasted_iota(
        jnp.int32, (kept_n, kept_n), 1
    )

    def column(row):
        return jnp.sum(jnp.where(eye, row, 0), axis=1, keepdims=True)

    lane_g = lax.broadcasted_iota(jnp.int32, (kept_n, 128), 1)
    sub_k = lax.broadcasted_iota(jnp.int32, (kept_n, 128), 0)
    hit = column(cohort_v[...]) == lane_g
    chosen = jnp.min(jnp.where(hit, sub_k, kept_n), axis=0, keepdims=True)
    row_v[0] = chosen
    to_smem = pltpu.make_async_copy(row_v.at[0], idx_s.at[0], row_sem.at[0])
    to_smem.start()
    slot_of = jnp.max(
        jnp.where(
            cohort_v[...] == lax.broadcasted_iota(jnp.int32, (groups, kept_n), 0),
            place_v[...] + 1,
            0,
        ),
        axis=1,
        keepdims=True,
    )
    meta_mine[...] = jnp.broadcast_to(slot_of, (groups, 128)).reshape(groups, 1, 128)

    for copy in ins[2:5]:
        copy.wait()
    steps = qb.shape[0]

    def spread_queries(which):
        for t in which:
            for h in range(heads):
                qf[pl.ds((t * heads + h) * cand, cand), :] = qb[
                    t, :, h * HD : (h + 1) * HD
                ].astype(jnp.float32)

    spread_queries(range(steps // 2, steps))
    for which, source in enumerate((nkb, nvb)):
        for t in range(steps):
            nf[which, pl.ds(t * cand, cand), :] = source[t].astype(jnp.float32)
        nf[which, pl.ds(steps * cand, (8 - steps) * cand), :] = jnp.zeros(
            ((8 - steps) * cand, HD), jnp.float32
        )
    empty = jnp.zeros((PAD - 8, HD), jnp.float32)
    for c in range(cand):
        for which, target in enumerate((kx, vx)):
            rows = nf[which, pl.ds(c, 8, stride=cand), :]
            target[c, pl.ds(cache, PAD), :] = jnp.concatenate([rows, empty], axis=0).astype(
                jnp.bfloat16
            )
    for copy in ins[5:]:
        copy.wait()

    width = cache + PAD
    lane = lax.broadcasted_iota(jnp.int32, (2 * heads, width), 1)
    step_of_row = lax.broadcasted_iota(jnp.int32, (2 * heads, width), 0) // heads
    rate = math.log2(math.e) / math.sqrt(HD)

    def attend(cands, first_step):
        fresh_seen = (lane >= cache) & (lane <= cache + first_step + step_of_row)
        scores = []
        for c in cands:
            q = jnp.concatenate(
                [
                    qf[pl.ds((first_step + i) * heads * cand + c, heads, stride=cand), :]
                    for i in range(2)
                ],
                axis=0,
            ).astype(jnp.bfloat16)
            s = lax.dot_general(q, kx[c], NT, preferred_element_type=jnp.float32)
            scores.append(jnp.where((lane < lengths_s[c]) | fresh_seen, s, NEG))
        tops = [jnp.max(s, axis=1, keepdims=True) for s in scores]
        weights = [jnp.exp2((s - m) * rate) for s, m in zip(scores, tops)]
        totals = [jnp.sum(w, axis=1, keepdims=True) for w in weights]
        return [
            jnp.dot(w.astype(jnp.bfloat16), vx[c], preferred_element_type=jnp.float32)
            / total
            for c, w, total in zip(cands, weights, totals)
        ]

    def late_block(b, _):
        cands = [kept_s[0, b * BLOCK + j] for j in range(BLOCK)]
        outs = attend(cands, steps // 2)
        for j, o in enumerate(outs):
            late_buf[b * BLOCK + j] = o.astype(jnp.bfloat16)
        return 0

    late_buf[kept_n] = jnp.zeros(late_buf.shape[1:], jnp.bfloat16)
    lax.fori_loop(0, kept_n // BLOCK, late_block, 0)

    to_smem.wait()
    for g in range(groups):
        send[g] = late_buf[idx_s[0, 0, g]]

    pl.semaphore_wait(barrier, groups - 1 + tn - 1)
    for g in others:
        pltpu.make_async_remote_copy(
            src_ref=meta_mine.at[g],
            dst_ref=meta_all.at[g_me],
            send_sem=meta_send,
            recv_sem=meta_recv,
            device_id=(g, t_me),
            device_id_type=MESH,
        ).start()
    for g in others:
        pltpu.make_async_remote_copy(
            src_ref=send.at[g],
            dst_ref=recv.at[g_me],
            send_sem=send_sem,
            recv_sem=recv_sem,
            device_id=(g, t_me),
            device_id_type=MESH,
        ).start()
    meta_all[g_me] = meta_mine[g_me]
    recv[g_me] = send[g_me]

    spread_queries(range(steps // 2))

    def early_block(b, _):
        cands = [b * BLOCK + j for j in range(BLOCK)]
        outs = attend(cands, 0)
        for c, o in zip(cands, outs):
            for i in range(2):
                of[pl.ds(i * heads * cand + c, heads, stride=cand), :] = o[
                    i * heads : (i + 1) * heads
                ]
        return 0

    lax.fori_loop(0, cand // BLOCK, early_block, 0)
    for t in range(2):
        for h in range(heads):
            stage[t, :, h * HD : (h + 1) * HD] = of[
                pl.ds((t * heads + h) * cand, cand), :
            ].astype(jnp.bfloat16)
    rw[t_me] = jnp.zeros(rw.shape[1:], jnp.float32)
    rw[t_me, :, pl.ds(0, cand)] = lax.dot_general(
        weight_v[...].reshape(1, heads * HD), stage[1], NT, preferred_element_type=jnp.float32
    )

    def rw_copy(d):
        return pltpu.make_async_remote_copy(
            src_ref=rw.at[t_me],
            dst_ref=rw.at[t_me],
            send_sem=rw_send,
            recv_sem=rw_recv,
            device_id=(g_me, lax.rem(t_me + d, tn)),
            device_id_type=MESH,
        )

    lax.fori_loop(1, tn, lambda d, _: (rw_copy(d).start(), 0)[1], 0)

    for sem in (meta_send, meta_recv):
        all_of(meta_all, groups - 1, sem).wait()
    slots_here = meta_all[...].reshape(groups, 128)
    lane_m = lax.broadcasted_iota(jnp.int32, (groups, 128), 1)
    sender = lax.broadcasted_iota(jnp.int32, (groups, 128), 0)
    row_v[1] = jnp.max(
        jnp.where(slots_here == lane_m + 1, sender, 0), axis=0, keepdims=True
    )
    back = pltpu.make_async_copy(row_v.at[1], idx_s.at[1], row_sem.at[1])
    back.start()
    back.wait()

    for sem in (send_sem, recv_sem):
        all_of(recv, groups - 1, sem).wait()
    for p in range(kept_n):
        o = recv[idx_s[1, 0, p]].astype(jnp.float32)
        for i in range(2):
            of[pl.ds(i * heads * kept_n + p, heads, stride=kept_n), :] = o[
                i * heads : (i + 1) * heads
            ]
    for t in range(2):
        for h in range(heads):
            late_stage[t, :, h * HD : (h + 1) * HD] = of[
                pl.ds((t * heads + h) * kept_n, kept_n), :
            ].astype(jnp.bfloat16)
    if tn > 1:
        for sem in (rw_send, rw_recv):
            all_of(rw, tn - 1, sem).wait()
    reward_o[...] = jnp.sum(rw[...], axis=0)[:, :cand]


def write_out(early_v, reward_v, late_v, early_h, reward_h, late_h, sems):
    copies = [
        pltpu.make_async_copy(src, dst, sems.at[i])
        for i, (src, dst) in enumerate(
            ((early_v, early_h), (late_v, late_h), (reward_v, reward_h))
        )
    ]
    for copy in copies:
        copy.start()
    for copy in copies:
        copy.wait()


def local(
    ring,
    tn,
    cache_keys,
    cache_values,
    lengths,
    queries,
    new_keys,
    new_values,
    reward_weight,
    kept_candidates,
    arrival_cohort,
    arrival_place,
):
    zn, yn = ring
    groups = zn * yn
    cand, cache, _ = cache_keys.shape
    steps, _, columns = queries.shape
    heads = columns // HD
    kept_n = kept_candidates.shape[1]
    half = steps // 2
    bf16, f32, i32 = jnp.bfloat16, jnp.float32, jnp.int32
    anywhere = pl.BlockSpec(memory_space=pl.ANY)
    dma = pltpu.SemaphoreType.DMA
    shapes = (
        ((half, cand, columns), bf16),
        ((1, cand), f32),
        ((half, kept_n, columns), bf16),
    )
    in_hbm = [
        pltpu.with_memory_space_constraint(x, pltpu.HBM)
        for x in (
            kept_candidates,
            lengths,
            arrival_cohort,
            arrival_place,
            reward_weight,
            cache_keys,
            cache_values,
            queries,
            new_keys,
            new_values,
        )
    ]
    staged = pl.pallas_call(
        functools.partial(kernel, (zn, yn, tn, cand, kept_n, heads)),
        out_shape=tuple(pltpu.VMEM(*shape) for shape in shapes),
        in_specs=[anywhere] * len(in_hbm),
        out_specs=(pl.BlockSpec(memory_space=pltpu.VMEM),) * 3,
        scratch_shapes=[
            pltpu.SMEM(kept_candidates.shape, i32),
            pltpu.SMEM(lengths.shape, i32),
            pltpu.VMEM(arrival_cohort.shape, i32),
            pltpu.VMEM(arrival_place.shape, i32),
            pltpu.VMEM(reward_weight.shape, bf16),
            pltpu.VMEM((cand, cache + PAD, HD), bf16),
            pltpu.VMEM((cand, cache + PAD, HD), bf16),
            pltpu.VMEM(queries.shape, bf16),
            pltpu.VMEM(new_keys.shape, bf16),
            pltpu.VMEM(new_values.shape, bf16),
            pltpu.VMEM((steps * heads * cand, HD), f32),
            pltpu.VMEM((2, 8 * cand, HD), f32),
            pltpu.VMEM((half * heads * cand, HD), f32),
            pltpu.VMEM((kept_n + 1, half * heads, HD), bf16),
            pltpu.VMEM((groups, half * heads, HD), bf16),
            pltpu.VMEM((groups, half * heads, HD), bf16),
            pltpu.VMEM((2, 1, 128), i32),
            pltpu.SMEM((2, 1, 128), i32),
            pltpu.VMEM((groups, 1, 128), i32),
            pltpu.VMEM((groups, 1, 128), i32),
            pltpu.VMEM((tn, 1, 128), f32),
            dma((len(in_hbm),)), dma((2,)),
            dma, dma, dma, dma, dma, dma,
        ],
        compiler_params=pltpu.CompilerParams(
            collective_id=0, has_side_effects=True, vmem_limit_bytes=40 * 1024 * 1024
        ),
    )(*in_hbm)
    early, reward, late = pl.pallas_call(
        write_out,
        out_shape=tuple(pltpu.HBM(*shape) for shape in shapes),
        in_specs=[anywhere] * 3,
        out_specs=(anywhere,) * 3,
        scratch_shapes=[dma((3,))],
        compiler_params=pltpu.CompilerParams(vmem_limit_bytes=2 * 1024 * 1024),
    )(*(pltpu.with_memory_space_constraint(x, pltpu.VMEM) for x in staged))
    return early, reward.reshape(cand), late


def solution(mesh):
    groups, tn = mesh.shape["dp"], mesh.shape["tensor"]
    yn = min(RING, groups)
    placed = (
        P("dp", None, "tensor"),
        P("dp", None, "tensor"),
        P("dp"),
        P(None, "dp", "tensor"),
        P(None, "dp", "tensor"),
        P(None, "dp", "tensor"),
        P("tensor"),
        P("dp", None),
        P("dp", None),
        P("dp", None),
    )
    return jax.shard_map(
        functools.partial(local, (groups // yn, yn), tn),
        mesh=mesh,
        in_specs=placed,
        out_specs=(P(None, "dp", "tensor"), P("dp"), P(None, "dp", "tensor")),
        check_vma=False,
    )
```

time: 38.2 us -> 27 us (0.71)
  Pallas kernels: 31.8 us -> 26.2 us
  local copies, waits for them, and re-layouts: 5.58 us -> 0 us
    pallas_call x1, Pallas kernels: 31.8 us -> 25.5 us  [local(): pl.pallas_call(functools.partial(kernel, (zn, yn, tn, cand, kept_n, heads...]
    unnamed x3 -> x0, local copies, waits for them, and re-layouts: 4.3 us -> none
    reshape x1 -> x0, local copies, waits for them, and re-layouts: 1.28 us -> none  [local(): reward_weight.reshape(1, columns)]
    pallas_call x0 -> x1, Pallas kernels: none -> 0.75 us  [local(): pl.pallas_call(write_out, out_shape=tuple((pltpu.HBM(*shape) for shape in...]
where the time goes in v2:
time: 27 us; the launch traced here: 26.9 us
  Pallas kernels  26.2 us (97%)
  between operations  0.64 us (2%)
    pallas_call x1, Pallas kernels, local(): pl.pallas_call(functools.partial(kernel, (zn, yn, tn, cand, kept_n, heads...  25.5 us
    pallas_call x1, Pallas kernels, local(): pl.pallas_call(write_out, out_shape=tuple((pltpu.HBM(*shape) for shape in...  0.75 us

profile of v2, /device:TPU:6, one launch (start us, length us, event | category | flops | bytes accessed | tf_op | source)
XLA Modules:
  0.0 26.9 jit_solution(11890810401669488328)
XLA Ops:
  0.6 25.5 %shard_map.121 = (bf16[2,48,1024]{2,1,0:T(8,128)(2,1)S(1)}, f32[1,48]{1,0:T(1,128)S(1)}, bf16[2,32,1024]{2,1,0:T(8,128)(2,1)S(1)}) custom-call(s32[1,32]{1,0:T(1,128)} %kept_h.1, s32[48]{0:T(128)} %lengths_h.1, s32[1,32]{1,0:T(1,128)} %cohort_h.1, s32[1,32]{1,0:T(1,128)} %place_h.1, bf16[1024]{0:T(1024)(128)(2,1)} %weight_h.1, bf16[48,128,128]{2,1,0:T(8,128)(2,1)} %keys_h.1, ...), custom_call_target="tpu_custom_call" | custom-call | tf_op jit(solution)/shard_map/pallas_call | solution.py:325
  26.1 0.8 %shard_map.122 = (bf16[2,48,1024]{2,1,0:T(8,128)(2,1)}, f32[1,48]{1,0:T(1,128)}, bf16[2,32,1024]{2,1,0:T(8,128)(2,1)}) custom-call(bf16[2,48,1024]{2,1,0:T(8,128)(2,1)S(1)} %get-tuple-element.9.early_v, f32[1,48]{1,0:T(1,128)S(1)} %get-tuple-element.10.reward_v, bf16[2,32,1024]{2,1,0:T(8,128)(2,1)S(1)} %get-tuple-element.11.late_v), custom_call_target="tpu_custom_call" | custom-call | tf_op jit(solution)/shard_map/pallas_call | solution.py:359

commit v3 on v2

--- a/solution.py
+++ b/solution.py
@@ -31,6 +31,7 @@
     kx, vx, qb, nkb, nvb, qf, nf, of, late_buf, send, recv,
     row_v, idx_s, meta_mine, meta_all, rw,
     in_sem, row_sem, send_sem, recv_sem, meta_send, meta_recv, rw_send, rw_recv,
+    ready_sem,
 ):
     zn, yn, tn, cand, kept_n, heads = dims
     groups = zn * yn
@@ -38,14 +39,6 @@
     g_me = lax.axis_index("dp")
     t_me = lax.axis_index("tensor")
     z_me, y_me = g_me // yn, g_me % yn
-
-    def hops(offset):
-        return min(offset[0], zn - offset[0]) + min(offset[1], yn - offset[1])
-
-    others = sorted(((i, j) for i in range(zn) for j in range(yn)), key=hops)[:0:-1]
-    others = [
-        lax.rem(z_me + i, zn) * yn + lax.rem(y_me + j, yn) for i, j in others
-    ]
 
     ins = [
         pltpu.make_async_copy(src, dst, in_sem.at[i])
@@ -69,8 +62,11 @@
 
     barrier = pltpu.get_barrier_semaphore()
 
-    for g in others:
+    def greet(g, _):
         pl.semaphore_signal(barrier, inc=1, device_id=(g, t_me), device_id_type=MESH)
+        return 0
+
+    lax.fori_loop(g_me + 1, groups, greet, 0)
 
     def greet_t(d, _):
         pl.semaphore_signal(
@@ -177,25 +173,37 @@
     for g in range(groups):
         send[g] = late_buf[idx_s[0, 0, g]]
 
-    pl.semaphore_wait(barrier, groups - 1 + tn - 1)
-    for g in others:
-        pltpu.make_async_remote_copy(
-            src_ref=meta_mine.at[g],
-            dst_ref=meta_all.at[g_me],
-            send_sem=meta_send,
-            recv_sem=meta_recv,
-            device_id=(g, t_me),
-            device_id_type=MESH,
-        ).start()
-    for g in others:
-        pltpu.make_async_remote_copy(
-            src_ref=send.at[g],
-            dst_ref=recv.at[g_me],
-            send_sem=send_sem,
-            recv_sem=recv_sem,
-            device_id=(g, t_me),
-            device_id_type=MESH,
-        ).start()
+    def send_to(g, _):
+        for src, dst, sem_here, sem_there in (
+            (meta_mine, meta_all, meta_send, meta_recv),
+            (send, recv, send_sem, recv_sem),
+        ):
+            pltpu.make_async_remote_copy(
+                src_ref=src.at[g],
+                dst_ref=dst.at[g_me],
+                send_sem=sem_here,
+                recv_sem=sem_there,
+                device_id=(g, t_me),
+                device_id_type=MESH,
+            ).start()
+        return 0
+
+    def tell(g, _):
+        pl.semaphore_signal(
+            ready_sem.at[z_me], inc=1, device_id=(g, t_me), device_id_type=MESH
+        )
+        return 0
+
+    if tn > 1:
+        pl.semaphore_wait(barrier, g_me + tn - 1)
+    else:
+
+        @pl.when(g_me > 0)
+        def _():
+            pl.semaphore_wait(barrier, g_me)
+
+    lax.fori_loop(0, g_me, send_to, 0)
+    lax.fori_loop(0, g_me, tell, 0)
     meta_all[g_me] = meta_mine[g_me]
     recv[g_me] = send[g_me]
 
@@ -233,6 +241,19 @@
         )
 
     lax.fori_loop(1, tn, lambda d, _: (rw_copy(d).start(), 0)[1], 0)
+
+    @pl.when(y_me < yn - 1)
+    def _():
+        pl.semaphore_wait(ready_sem.at[z_me], yn - 1 - y_me)
+        lax.fori_loop(g_me + 1, (z_me + 1) * yn, send_to, 0)
+
+    def later_plane(z, _):
+        pl.semaphore_wait(ready_sem.at[z], yn)
+        for y in range(yn):
+            send_to(z * yn + y, 0)
+        return 0
+
+    lax.fori_loop(z_me + 1, zn, later_plane, 0)
 
     for sem in (meta_send, meta_recv):
         all_of(meta_all, groups - 1, sem).wait()
@@ -351,6 +372,7 @@
             pltpu.VMEM((tn, 1, 128), f32),
             dma((len(in_hbm),)), dma((2,)),
             dma, dma, dma, dma, dma, dma,
+            pltpu.SemaphoreType.REGULAR((zn,)),
         ],
         compiler_params=pltpu.CompilerParams(
             collective_id=0, has_side_effects=True, vmem_limit_bytes=40 * 1024 * 1024

time: 27 us -> 24.8 us (0.919)
  Pallas kernels: 26.2 us -> 24 us
    pallas_call x1, Pallas kernels: 25.5 us -> 23.3 us  [local(): pl.pallas_call(functools.partial(kernel, (zn, yn, tn, cand, kept_n, heads...]
where the time goes in v3:
time: 24.8 us; the launch traced here: 24.7 us
  Pallas kernels  24 us (97%)
  between operations  0.64 us (3%)
    pallas_call x1, Pallas kernels, local(): pl.pallas_call(functools.partial(kernel, (zn, yn, tn, cand, kept_n, heads...  23.3 us
    pallas_call x1, Pallas kernels, local(): pl.pallas_call(write_out, out_shape=tuple((pltpu.HBM(*shape) for shape in...  0.75 us

profile of v3, /device:TPU:6, one launch (start us, length us, event | category | flops | bytes accessed | tf_op | source)
XLA Modules:
  0.0 24.7 jit_solution(7813998426605222208)
XLA Ops:
  0.6 23.3 %shard_map.121 = (bf16[2,48,1024]{2,1,0:T(8,128)(2,1)S(1)}, f32[1,48]{1,0:T(1,128)S(1)}, bf16[2,32,1024]{2,1,0:T(8,128)(2,1)S(1)}) custom-call(s32[1,32]{1,0:T(1,128)} %kept_h.1, s32[48]{0:T(128)} %lengths_h.1, s32[1,32]{1,0:T(1,128)} %cohort_h.1, s32[1,32]{1,0:T(1,128)} %place_h.1, bf16[1024]{0:T(1024)(128)(2,1)} %weight_h.1, bf16[48,128,128]{2,1,0:T(8,128)(2,1)} %keys_h.1, ...), custom_call_target="tpu_custom_call" | custom-call | tf_op jit(solution)/shard_map/pallas_call | solution.py:346
  23.9 0.8 %shard_map.122 = (bf16[2,48,1024]{2,1,0:T(8,128)(2,1)}, f32[1,48]{1,0:T(1,128)}, bf16[2,32,1024]{2,1,0:T(8,128)(2,1)}) custom-call(bf16[2,48,1024]{2,1,0:T(8,128)(2,1)S(1)} %get-tuple-element.9.early_v, f32[1,48]{1,0:T(1,128)S(1)} %get-tuple-element.10.reward_v, bf16[2,32,1024]{2,1,0:T(8,128)(2,1)S(1)} %get-tuple-element.11.late_v), custom_call_target="tpu_custom_call" | custom-call | tf_op jit(solution)/shard_map/pallas_call | solution.py:381

commit v4 on v3

--- a/solution.py
+++ b/solution.py
@@ -29,7 +29,7 @@
     stage, reward_o, late_stage,
     kept_s, lengths_s, cohort_v, place_v, weight_v,
     kx, vx, qb, nkb, nvb, qf, nf, of, late_buf, send, recv,
-    row_v, idx_s, meta_mine, meta_all, rw,
+    spread, row_v, idx_s, meta_mine, meta_all, rw,
     in_sem, row_sem, send_sem, recv_sem, meta_send, meta_recv, rw_send, rw_recv,
     ready_sem,
 ):
@@ -90,8 +90,8 @@
     sub_k = lax.broadcasted_iota(jnp.int32, (kept_n, 128), 0)
     hit = column(cohort_v[...]) == lane_g
     chosen = jnp.min(jnp.where(hit, sub_k, kept_n), axis=0, keepdims=True)
-    row_v[0] = chosen
-    to_smem = pltpu.make_async_copy(row_v.at[0], idx_s.at[0], row_sem.at[0])
+    row_v[...] = chosen
+    to_smem = pltpu.make_async_copy(row_v, idx_s, row_sem)
     to_smem.start()
     slot_of = jnp.max(
         jnp.where(
@@ -171,7 +171,7 @@
 
     to_smem.wait()
     for g in range(groups):
-        send[g] = late_buf[idx_s[0, 0, g]]
+        send[g] = late_buf[idx_s[0, g]]
 
     def send_to(g, _):
         for src, dst, sem_here, sem_there in (
@@ -202,7 +202,27 @@
         def _():
             pl.semaphore_wait(barrier, g_me)
 
-    lax.fori_loop(0, g_me, send_to, 0)
+    def turn(j):
+        return lax.rem(y_me + z_me + j, yn)
+
+    def to_planes(*planes):
+        for j in range(yn):
+            for z in planes:
+                send_to(z * yn + turn(j), 0)
+
+    def to_plane(z, _):
+        to_planes(z)
+        return 0
+
+    half = zn // 2
+
+    @pl.when(z_me >= half)
+    def _():
+        for a in range(0, half, 2):
+            to_planes(*range(a, min(a + 2, half)))
+
+    lax.fori_loop(jnp.where(z_me >= half, half, 0), z_me, to_plane, 0)
+    lax.fori_loop(z_me * yn, g_me, send_to, 0)
     lax.fori_loop(0, g_me, tell, 0)
     meta_all[g_me] = meta_mine[g_me]
     recv[g_me] = send[g_me]
@@ -249,37 +269,27 @@
 
     def later_plane(z, _):
         pl.semaphore_wait(ready_sem.at[z], yn)
-        for y in range(yn):
-            send_to(z * yn + y, 0)
-        return 0
+        return to_plane(z, 0)
 
     lax.fori_loop(z_me + 1, zn, later_plane, 0)
 
     for sem in (meta_send, meta_recv):
         all_of(meta_all, groups - 1, sem).wait()
-    slots_here = meta_all[...].reshape(groups, 128)
-    lane_m = lax.broadcasted_iota(jnp.int32, (groups, 128), 1)
-    sender = lax.broadcasted_iota(jnp.int32, (groups, 128), 0)
-    row_v[1] = jnp.max(
-        jnp.where(slots_here == lane_m + 1, sender, 0), axis=0, keepdims=True
-    )
-    back = pltpu.make_async_copy(row_v.at[1], idx_s.at[1], row_sem.at[1])
-    back.start()
-    back.wait()
-
-    for sem in (send_sem, recv_sem):
-        all_of(recv, groups - 1, sem).wait()
-    for p in range(kept_n):
-        o = recv[idx_s[1, 0, p]].astype(jnp.float32)
-        for i in range(2):
-            of[pl.ds(i * heads * kept_n + p, heads, stride=kept_n), :] = o[
-                i * heads : (i + 1) * heads
-            ]
+    slots_here = meta_all[...].reshape(groups, 128)[:, :kept_n]
+    slot_ids = lax.broadcasted_iota(jnp.int32, (groups, kept_n), 1) + 1
+    place = (slots_here == slot_ids).astype(jnp.float32).astype(jnp.bfloat16)
+    all_of(recv, groups - 1, recv_sem).wait()
+    spread[...] = recv[...].reshape(groups * 2 * heads, HD).astype(jnp.float32)
     for t in range(2):
         for h in range(heads):
-            late_stage[t, :, h * HD : (h + 1) * HD] = of[
-                pl.ds((t * heads + h) * kept_n, kept_n), :
-            ].astype(jnp.bfloat16)
+            rows = spread[pl.ds(t * heads + h, groups, stride=2 * heads), :]
+            late_stage[t, :, h * HD : (h + 1) * HD] = lax.dot_general(
+                place,
+                rows.astype(jnp.bfloat16),
+                (((0,), (0,)), ((), ())),
+                preferred_element_type=jnp.float32,
+            ).astype(jnp.bfloat16)
+    all_of(recv, groups - 1, send_sem).wait()
     if tn > 1:
         for sem in (rw_send, rw_recv):
             all_of(rw, tn - 1, sem).wait()
@@ -365,12 +375,13 @@
             pltpu.VMEM((kept_n + 1, half * heads, HD), bf16),
             pltpu.VMEM((groups, half * heads, HD), bf16),
             pltpu.VMEM((groups, half * heads, HD), bf16),
-            pltpu.VMEM((2, 1, 128), i32),
-            pltpu.SMEM((2, 1, 128), i32),
+            pltpu.VMEM((groups * half * heads, HD), f32),
+            pltpu.VMEM((1, 128), i32),
+            pltpu.SMEM((1, 128), i32),
             pltpu.VMEM((groups, 1, 128), i32),
             pltpu.VMEM((groups, 1, 128), i32),
             pltpu.VMEM((tn, 1, 128), f32),
-            dma((len(in_hbm),)), dma((2,)),
+            dma((len(in_hbm),)), dma,
             dma, dma, dma, dma, dma, dma,
             pltpu.SemaphoreType.REGULAR((zn,)),
         ],

time: 24.8 us -> 24.1 us (0.972)
  Pallas kernels: 24 us -> 23.3 us
    pallas_call x1, Pallas kernels: 23.3 us -> 22.5 us  [local(): pl.pallas_call(functools.partial(kernel, (zn, yn, tn, cand, kept_n, heads...]
where the time goes in v4:
time: 24.1 us; the launch traced here: 23.9 us
  Pallas kernels  23.3 us (97%)
  between operations  0.64 us (3%)
    pallas_call x1, Pallas kernels, local(): pl.pallas_call(functools.partial(kernel, (zn, yn, tn, cand, kept_n, heads...  22.5 us
    pallas_call x1, Pallas kernels, local(): pl.pallas_call(write_out, out_shape=tuple((pltpu.HBM(*shape) for shape in...  0.75 us

profile of v4, /device:TPU:6, one launch (start us, length us, event | category | flops | bytes accessed | tf_op | source)
XLA Modules:
  0.0 23.9 jit_solution(7589297015502228001)
XLA Ops:
  0.6 22.5 %shard_map.121 = (bf16[2,48,1024]{2,1,0:T(8,128)(2,1)S(1)}, f32[1,48]{1,0:T(1,128)S(1)}, bf16[2,32,1024]{2,1,0:T(8,128)(2,1)S(1)}) custom-call(s32[1,32]{1,0:T(1,128)} %kept_h.1, s32[48]{0:T(128)} %lengths_h.1, s32[1,32]{1,0:T(1,128)} %cohort_h.1, s32[1,32]{1,0:T(1,128)} %place_h.1, bf16[1024]{0:T(1024)(128)(2,1)} %weight_h.1, bf16[48,128,128]{2,1,0:T(8,128)(2,1)} %keys_h.1, ...), custom_call_target="tpu_custom_call" | custom-call | tf_op jit(solution)/shard_map/pallas_call | solution.py:356
  23.2 0.8 %shard_map.122 = (bf16[2,48,1024]{2,1,0:T(8,128)(2,1)}, f32[1,48]{1,0:T(1,128)}, bf16[2,32,1024]{2,1,0:T(8,128)(2,1)}) custom-call(bf16[2,48,1024]{2,1,0:T(8,128)(2,1)S(1)} %get-tuple-element.9.early_v, f32[1,48]{1,0:T(1,128)S(1)} %get-tuple-element.10.reward_v, bf16[2,32,1024]{2,1,0:T(8,128)(2,1)S(1)} %get-tuple-element.11.late_v), custom_call_target="tpu_custom_call" | custom-call | tf_op jit(solution)/shard_map/pallas_call | solution.py:392

commit v5 on v4

--- a/solution.py
+++ b/solution.py
@@ -11,7 +11,7 @@
 MESH = pl.DeviceIdType.MESH
 HD = 128
 PAD = 16
-BLOCK = 8
+BLOCK = 16
 RING = 8
 NEG = -1e30
 NT = (((1,), (1,)), ((), ()))
@@ -40,6 +40,23 @@
     t_me = lax.axis_index("tensor")
     z_me, y_me = g_me // yn, g_me % yn
 
+    half = zn // 2
+    depth = zn - half
+    late = z_me >= half
+    k_me = jnp.where(2 * y_me > yn, 2 * (yn - y_me), jnp.where(y_me > 0, 2 * y_me - 1, 0))
+    r_me = jnp.where(late, half * yn + k_me * depth + z_me - half, g_me)
+    b_me = jnp.where(late, half + k_me, z_me)
+    k_next = jnp.where(late, k_me + 1, 0)
+
+    def column_of(k, visit):
+        y = jnp.where(lax.rem(k, 2) == 1, (k + 1) // 2, lax.rem(yn - k // 2, yn))
+        for z in range(half, zn):
+            visit(z * yn + y, 0)
+        return 0
+
+    def in_column(visit):
+        return lambda z, _: visit(z * yn + y_me, 0)
+
     ins = [
         pltpu.make_async_copy(src, dst, in_sem.at[i])
         for i, (src, dst) in enumerate(
@@ -66,7 +83,9 @@
         pl.semaphore_signal(barrier, inc=1, device_id=(g, t_me), device_id_type=MESH)
         return 0
 
-    lax.fori_loop(g_me + 1, groups, greet, 0)
+    lax.fori_loop(g_me + 1, jnp.where(late, g_me + 1, half * yn), greet, 0)
+    lax.fori_loop(jnp.where(late, z_me + 1, zn), zn, in_column(greet), 0)
+    lax.fori_loop(k_next, yn, lambda k, _: column_of(k, greet), 0)
 
     def greet_t(d, _):
         pl.semaphore_signal(
@@ -190,17 +209,17 @@
 
     def tell(g, _):
         pl.semaphore_signal(
-            ready_sem.at[z_me], inc=1, device_id=(g, t_me), device_id_type=MESH
+            ready_sem.at[b_me], inc=1, device_id=(g, t_me), device_id_type=MESH
         )
         return 0
 
     if tn > 1:
-        pl.semaphore_wait(barrier, g_me + tn - 1)
+        pl.semaphore_wait(barrier, r_me + tn - 1)
     else:
 
-        @pl.when(g_me > 0)
+        @pl.when(r_me > 0)
         def _():
-            pl.semaphore_wait(barrier, g_me)
+            pl.semaphore_wait(barrier, r_me)
 
     def turn(j):
         return lax.rem(y_me + z_me + j, yn)
@@ -214,16 +233,19 @@
         to_planes(z)
         return 0
 
-    half = zn // 2
-
-    @pl.when(z_me >= half)
+    @pl.when(late)
     def _():
-        for a in range(0, half, 2):
-            to_planes(*range(a, min(a + 2, half)))
-
-    lax.fori_loop(jnp.where(z_me >= half, half, 0), z_me, to_plane, 0)
-    lax.fori_loop(z_me * yn, g_me, send_to, 0)
-    lax.fori_loop(0, g_me, tell, 0)
+        for a in range(half):
+            to_planes(a)
+
+    lax.fori_loop(0, jnp.where(late, 0, z_me), to_plane, 0)
+    lax.fori_loop(jnp.where(late, g_me, z_me * yn), g_me, send_to, 0)
+    lax.fori_loop(0, k_next - 1, lambda k, _: column_of(k, send_to), 0)
+    lax.fori_loop(half, jnp.where(late, z_me, half), in_column(send_to), 0)
+
+    lax.fori_loop(0, jnp.where(late, half * yn, g_me), tell, 0)
+    lax.fori_loop(0, k_next - 1, lambda k, _: column_of(k, tell), 0)
+    lax.fori_loop(half, jnp.where(late, z_me, half), in_column(tell), 0)
     meta_all[g_me] = meta_mine[g_me]
     recv[g_me] = send[g_me]
 
@@ -262,16 +284,29 @@
 
     lax.fori_loop(1, tn, lambda d, _: (rw_copy(d).start(), 0)[1], 0)
 
-    @pl.when(y_me < yn - 1)
+    @pl.when(jnp.logical_not(late))
     def _():
-        pl.semaphore_wait(ready_sem.at[z_me], yn - 1 - y_me)
-        lax.fori_loop(g_me + 1, (z_me + 1) * yn, send_to, 0)
-
-    def later_plane(z, _):
-        pl.semaphore_wait(ready_sem.at[z], yn)
-        return to_plane(z, 0)
-
-    lax.fori_loop(z_me + 1, zn, later_plane, 0)
+        @pl.when(y_me < yn - 1)
+        def _():
+            pl.semaphore_wait(ready_sem.at[z_me], yn - 1 - y_me)
+            lax.fori_loop(g_me + 1, (z_me + 1) * yn, send_to, 0)
+
+        def later_plane(z, _):
+            pl.semaphore_wait(ready_sem.at[z], yn)
+            return to_plane(z, 0)
+
+        lax.fori_loop(z_me + 1, half, later_plane, 0)
+
+    @pl.when(late & (z_me < zn - 1))
+    def _():
+        pl.semaphore_wait(ready_sem.at[half + k_me], zn - 1 - z_me)
+        lax.fori_loop(z_me + 1, zn, in_column(send_to), 0)
+
+    def later_column(k, _):
+        pl.semaphore_wait(ready_sem.at[half + k], depth)
+        return column_of(k, send_to)
+
+    lax.fori_loop(k_next, yn, later_column, 0)
 
     for sem in (meta_send, meta_recv):
         all_of(meta_all, groups - 1, sem).wait()
@@ -383,7 +418,7 @@
             pltpu.VMEM((tn, 1, 128), f32),
             dma((len(in_hbm),)), dma,
             dma, dma, dma, dma, dma, dma,
-            pltpu.SemaphoreType.REGULAR((zn,)),
+            pltpu.SemaphoreType.REGULAR((zn // 2 + yn,)),
         ],
         compiler_params=pltpu.CompilerParams(
             collective_id=0, has_side_effects=True, vmem_limit_bytes=40 * 1024 * 1024

time: 24.1 us -> 23.4 us (0.971)
  Pallas kernels: 23.3 us -> 22.6 us
    pallas_call x1, Pallas kernels: 22.5 us -> 21.9 us  [local(): pl.pallas_call(functools.partial(kernel, (zn, yn, tn, cand, kept_n, heads...]
where the time goes in v5:
time: 23.4 us; the launch traced here: 23.3 us
  Pallas kernels  22.6 us (97%)
  between operations  0.64 us (3%)
    pallas_call x1, Pallas kernels, local(): pl.pallas_call(functools.partial(kernel, (zn, yn, tn, cand, kept_n, heads...  21.9 us
    pallas_call x1, Pallas kernels, local(): pl.pallas_call(write_out, out_shape=tuple((pltpu.HBM(*shape) for shape in...  0.75 us

profile of v5, /device:TPU:6, one launch (start us, length us, event | category | flops | bytes accessed | tf_op | source)
XLA Modules:
  0.0 23.3 jit_solution(15729667647311368024)
XLA Ops:
  0.6 21.9 %shard_map.121 = (bf16[2,48,1024]{2,1,0:T(8,128)(2,1)S(1)}, f32[1,48]{1,0:T(1,128)S(1)}, bf16[2,32,1024]{2,1,0:T(8,128)(2,1)S(1)}) custom-call(s32[1,32]{1,0:T(1,128)} %kept_h.1, s32[48]{0:T(128)} %lengths_h.1, s32[1,32]{1,0:T(1,128)} %cohort_h.1, s32[1,32]{1,0:T(1,128)} %place_h.1, bf16[1024]{0:T(1024)(128)(2,1)} %weight_h.1, bf16[48,128,128]{2,1,0:T(8,128)(2,1)} %keys_h.1, ...), custom_call_target="tpu_custom_call" | custom-call | tf_op jit(solution)/shard_map/pallas_call | solution.py:391
  22.5 0.8 %shard_map.122 = (bf16[2,48,1024]{2,1,0:T(8,128)(2,1)}, f32[1,48]{1,0:T(1,128)}, bf16[2,32,1024]{2,1,0:T(8,128)(2,1)}) custom-call(bf16[2,48,1024]{2,1,0:T(8,128)(2,1)S(1)} %get-tuple-element.9.early_v, f32[1,48]{1,0:T(1,128)S(1)} %get-tuple-element.10.reward_v, bf16[2,32,1024]{2,1,0:T(8,128)(2,1)S(1)} %get-tuple-element.11.late_v), custom_call_target="tpu_custom_call" | custom-call | tf_op jit(solution)/shard_map/pallas_call | solution.py:427

commit v6 on v5

--- a/solution.py
+++ b/solution.py
@@ -31,7 +31,7 @@
     kx, vx, qb, nkb, nvb, qf, nf, of, late_buf, send, recv,
     spread, row_v, idx_s, meta_mine, meta_all, rw,
     in_sem, row_sem, send_sem, recv_sem, meta_send, meta_recv, rw_send, rw_recv,
-    ready_sem,
+    ready_sem, peer_sem,
 ):
     zn, yn, tn, cand, kept_n, heads = dims
     groups = zn * yn
@@ -77,6 +77,12 @@
     for copy in ins:
         copy.start()
 
+    pairs = (tn + 1) // 2
+    p_me = lax.rem(t_me, 2) * pairs + t_me // 2
+
+    def peer(p):
+        return (g_me, lax.rem(p, pairs) * 2 + p // pairs)
+
     barrier = pltpu.get_barrier_semaphore()
 
     def greet(g, _):
@@ -87,13 +93,11 @@
     lax.fori_loop(jnp.where(late, z_me + 1, zn), zn, in_column(greet), 0)
     lax.fori_loop(k_next, yn, lambda k, _: column_of(k, greet), 0)
 
-    def greet_t(d, _):
-        pl.semaphore_signal(
-            barrier, inc=1, device_id=(g_me, lax.rem(t_me + d, tn)), device_id_type=MESH
-        )
-        return 0
-
-    lax.fori_loop(1, tn, greet_t, 0)
+    def greet_peer(p, _):
+        pl.semaphore_signal(barrier, inc=1, device_id=peer(p), device_id_type=MESH)
+        return 0
+
+    lax.fori_loop(p_me + 1, tn, greet_peer, 0)
 
     for copy in ins[:2]:
         copy.wait()
@@ -213,13 +217,9 @@
         )
         return 0
 
-    if tn > 1:
-        pl.semaphore_wait(barrier, r_me + tn - 1)
-    else:
-
-        @pl.when(r_me > 0)
-        def _():
-            pl.semaphore_wait(barrier, r_me)
+    @pl.when(r_me + p_me > 0)
+    def _():
+        pl.semaphore_wait(barrier, r_me + p_me)
 
     def turn(j):
         return lax.rem(y_me + z_me + j, yn)
@@ -246,6 +246,11 @@
     lax.fori_loop(0, jnp.where(late, half * yn, g_me), tell, 0)
     lax.fori_loop(0, k_next - 1, lambda k, _: column_of(k, tell), 0)
     lax.fori_loop(half, jnp.where(late, z_me, half), in_column(tell), 0)
+    def tell_peer(p, _):
+        pl.semaphore_signal(peer_sem, inc=1, device_id=peer(p), device_id_type=MESH)
+        return 0
+
+    lax.fori_loop(0, p_me, tell_peer, 0)
     meta_all[g_me] = meta_mine[g_me]
     recv[g_me] = send[g_me]
 
@@ -272,17 +277,23 @@
         weight_v[...].reshape(1, heads * HD), stage[1], NT, preferred_element_type=jnp.float32
     )
 
-    def rw_copy(d):
-        return pltpu.make_async_remote_copy(
+    def send_reward(p, _):
+        pltpu.make_async_remote_copy(
             src_ref=rw.at[t_me],
             dst_ref=rw.at[t_me],
             send_sem=rw_send,
             recv_sem=rw_recv,
-            device_id=(g_me, lax.rem(t_me + d, tn)),
+            device_id=peer(p),
             device_id_type=MESH,
-        )
-
-    lax.fori_loop(1, tn, lambda d, _: (rw_copy(d).start(), 0)[1], 0)
+        ).start()
+        return 0
+
+    lax.fori_loop(0, p_me, send_reward, 0)
+
+    @pl.when(p_me < tn - 1)
+    def _():
+        pl.semaphore_wait(peer_sem, tn - 1 - p_me)
+        lax.fori_loop(p_me + 1, tn, send_reward, 0)
 
     @pl.when(jnp.logical_not(late))
     def _():
@@ -419,6 +430,7 @@
             dma((len(in_hbm),)), dma,
             dma, dma, dma, dma, dma, dma,
             pltpu.SemaphoreType.REGULAR((zn // 2 + yn,)),
+            pltpu.SemaphoreType.REGULAR,
         ],
         compiler_params=pltpu.CompilerParams(
             collective_id=0, has_side_effects=True, vmem_limit_bytes=40 * 1024 * 1024

time: 23.4 us -> 23.4 us (level)
  no operation moved by 1% of the time
where the time goes in v6:
time: 23.4 us; the launch traced here: 23.3 us
  Pallas kernels  22.6 us (97%)
  between operations  0.64 us (3%)
    pallas_call x1, Pallas kernels, local(): pl.pallas_call(functools.partial(kernel, (zn, yn, tn, cand, kept_n, heads...  21.9 us
    pallas_call x1, Pallas kernels, local(): pl.pallas_call(write_out, out_shape=tuple((pltpu.HBM(*shape) for shape in...  0.75 us

profile of v6, /device:TPU:6, one launch (start us, length us, event | category | flops | bytes accessed | tf_op | source)
XLA Modules:
  0.0 23.3 jit_solution(17254778504778924292)
XLA Ops:
  0.6 21.9 %shard_map.121 = (bf16[2,48,1024]{2,1,0:T(8,128)(2,1)S(1)}, f32[1,48]{1,0:T(1,128)S(1)}, bf16[2,32,1024]{2,1,0:T(8,128)(2,1)S(1)}) custom-call(s32[1,32]{1,0:T(1,128)} %kept_h.1, s32[48]{0:T(128)} %lengths_h.1, s32[1,32]{1,0:T(1,128)} %cohort_h.1, s32[1,32]{1,0:T(1,128)} %place_h.1, bf16[1024]{0:T(1024)(128)(2,1)} %weight_h.1, bf16[48,128,128]{2,1,0:T(8,128)(2,1)} %keys_h.1, ...), custom_call_target="tpu_custom_call" | custom-call | tf_op jit(solution)/shard_map/pallas_call | solution.py:402
  22.5 0.8 %shard_map.122 = (bf16[2,48,1024]{2,1,0:T(8,128)(2,1)}, f32[1,48]{1,0:T(1,128)}, bf16[2,32,1024]{2,1,0:T(8,128)(2,1)}) custom-call(bf16[2,48,1024]{2,1,0:T(8,128)(2,1)S(1)} %get-tuple-element.9.early_v, f32[1,48]{1,0:T(1,128)S(1)} %get-tuple-element.10.reward_v, bf16[2,32,1024]{2,1,0:T(8,128)(2,1)S(1)} %get-tuple-element.11.late_v), custom_call_target="tpu_custom_call" | custom-call | tf_op jit(solution)/shard_map/pallas_call | solution.py:439
